TPU v7x, 32 devices: a whole 2x2x4 slice. The times are simulated.
32 devices in a mesh: slab: 8 (over z, y), beam: 4 (over x, core).
Axes of the slice: x: 2, y: 2, z: 4, core: 2. Of those that a mesh axis runs over, the one named last changes fastest.
Arguments:
- traces: bfloat16 [512, 128, 1024], P(('slab', 'beam')), may hold values from -6 to 6
- shot_window: int32 [512], P(('slab', 'beam')), may hold values from 0 to 15, as said below
- trace_slot: int32 [512, 128], P(('slab', 'beam')), may hold values from 0 to 63
- ray_phase: bfloat16 [256, 1024], replicated, may hold values from -0.1875 to 0.1875
- ray_index: int32 [16, 192], P('beam', 'slab'), may hold values from 0 to 255
- beam_basis: bfloat16 [2, 1024, 8192], P(None, 'beam'), may hold values from -0.125 to 0.125
Outputs:
- image: float32 [192, 8192], P('slab', 'beam')
Inputs may be any that keep to these rules, and one draw needn't show every extreme that they name: `shot_window`: within each aligned block of 16 shots (the shots of one device), for every beam owner b exactly 4 shots name a window w with w // 4 = b.
All inputs are finite; a program needn't handle non-finite values.
Results may differ from a plain program's by a relative error of at most 0.0041.
Values may be sent and summed in bfloat16 or wider, within the bound.
A program may use at most 64 MiB of HBM per device.

v0:
```python
import math

import jax
import jax.numpy as jnp
from jax import lax
from jax.sharding import PartitionSpec as P

P_SIZE = 64
K = 64
WIN_OWN = 4


def slant_tables():
    phase_steps = (
        jnp.arange(P_SIZE, dtype=jnp.int32)[:, None] * jnp.arange(K, dtype=jnp.int32)[None, :] % K
    )
    angles = phase_steps.astype(jnp.float32) * jnp.float32(2.0 * math.pi / K)
    return (jnp.cos(angles), jnp.sin(angles))


def slant_stack(binned, cosine_table, sine_table):
    freq_count = binned.shape[-1] // 2
    real_part = binned[..., :freq_count]
    imag_part = binned[..., freq_count:]
    high = lax.Precision.HIGHEST
    panel_re = jnp.einsum("ps,wsf->wpf", cosine_table, real_part, precision=high) + jnp.einsum(
        "ps,wsf->wpf", sine_table, imag_part, precision=high
    )
    panel_im = jnp.einsum("ps,wsf->wpf", cosine_table, imag_part, precision=high) - jnp.einsum(
        "ps,wsf->wpf", sine_table, real_part, precision=high
    )
    return jnp.concatenate([panel_re, panel_im], axis=-1)


def bin_traces(samples, labels, wanted):
    binning = (wanted[:, None] == labels[None, :]).astype(jnp.bfloat16)
    return jnp.dot(binning, samples, preferred_element_type=jnp.float32)


def body(traces, shot_window, trace_slot, ray_phase, ray_index, beam_basis):
    shot_count, per_shot, doubled = traces.shape
    freq_count = doubled // 2
    beam_count = lax.axis_size("beam")
    slab_count = lax.axis_size("slab")
    stack_scale = (shot_count * slab_count * beam_count * per_shot / (WIN_OWN * beam_count)) ** (
        -0.5
    )
    cosine_table, sine_table = slant_tables()
    labels = jnp.repeat(shot_window, per_shot) * K + trace_slot.reshape(-1)
    samples = traces.reshape(-1, doubled)
    window_count = WIN_OWN * P_SIZE * lax.axis_size("beam") // P_SIZE
    wanted = jnp.arange(window_count * K, dtype=jnp.int32)
    binned = bin_traces(samples, labels, wanted)
    stacked = slant_stack(binned.reshape(window_count, K, doubled), cosine_table, sine_table)
    partial_value = lax.psum_scatter(
        stacked.reshape(WIN_OWN * P_SIZE * lax.axis_size("beam"), doubled)
        * jnp.float32(stack_scale),
        "beam",
        scatter_dimension=0,
        tiled=True,
    )
    beam_panel = lax.psum(partial_value, "slab").astype(jnp.bfloat16)
    ray_count = ray_phase.shape[0]
    depths = ray_index.shape[1]
    ray_pick = (
        ray_index.reshape(-1)[:, None] == jnp.arange(ray_count, dtype=jnp.int32)[None, :]
    ).astype(jnp.bfloat16)
    rays = jnp.dot(ray_pick, ray_phase, preferred_element_type=jnp.float32).astype(jnp.bfloat16)
    rays = rays.reshape(WIN_OWN, depths, doubled)
    panel_three = beam_panel.reshape(WIN_OWN, P_SIZE, doubled)
    panel_re = panel_three[..., :freq_count]
    panel_im = panel_three[..., freq_count:]
    left_re = jnp.concatenate([panel_re, -panel_im], axis=-1)
    left_im = jnp.concatenate([panel_im, panel_re], axis=-1)
    wave_re = jnp.einsum("wzf,wpf->zwp", rays, left_re, preferred_element_type=jnp.float32).astype(
        jnp.bfloat16
    )
    wave_im = jnp.einsum("wzf,wpf->zwp", rays, left_im, preferred_element_type=jnp.float32).astype(
        jnp.bfloat16
    )
    mixture = jnp.concatenate(
        [wave_re.reshape(depths, WIN_OWN * P_SIZE), -wave_im.reshape(depths, WIN_OWN * P_SIZE)],
        axis=1,
    )
    basis_rows = beam_basis.reshape(2 * WIN_OWN * P_SIZE, beam_basis.shape[2])
    image_part = jnp.dot(mixture, basis_rows, preferred_element_type=jnp.float32)
    return lax.psum_scatter(image_part, "beam", scatter_dimension=1, tiled=True)


def solution(mesh):
    in_specs = (
        P(("slab", "beam"), None, None),
        P(("slab", "beam")),
        P(("slab", "beam"), None),
        P(),
        P("beam", "slab"),
        P(None, "beam", None),
    )
    out_specs = P("slab", "beam")
    return jax.shard_map(body, mesh=mesh, in_specs=in_specs, out_specs=out_specs, check_vma=False)
```

profile of v0, /device:TPU:0, one launch (start us, length us, event | category | flops | bytes accessed | tf_op | source)
XLA Modules:
  0.0 180.6 jit_solution(7354465982065974680)
XLA Ops:
  6.5 0.0 copy-start
  6.5 0.0 reduce-scatter.3.cloned.1.call-start
  6.5 0.7 broadcast_multiply_fusion
  7.3 0.8 add_bitcast_fusion.1
  8.0 6.4 %fusion = f32[16,64,1024]{2,1,0:T(8,128)S(1)} fusion(bf16[2048,1024,1]{1,0,2:T(8,128)(2,1)} %bitcast.37, s32[2048]{0:T(1024)S(1)} %add_bitcast_fusion.1, s32[16,64]{1,0:T(8,128)S(1)} %multiply_add_fusion), kind=kOutput, calls=%fused_computation | convolution fusion | flops 4297064448 | bytes 8400896 | tf_op jit(solution)/shard_map/dot_general | solution.py:37
  14.4 2.3 %fusion.6 = f32[16,512,64]{1,2,0:T(8,128)S(1)} fusion(f32[16,64,1024]{2,1,0:T(8,128)S(1)} %fusion), kind=kOutput, calls=%fused_computation.9 | convolution fusion | flops 402710528 | bytes 4194304 | tf_op jit(solution)/shard_map/ps,wsf->wpf/dot_general | solution.py:26
  16.7 2.3 %fusion.4 = f32[16,512,64]{1,2,0:T(8,128)S(1)} fusion(f32[16,64,1024]{2,1,0:T(8,128)S(1)} %fusion), kind=kOutput, calls=%fused_computation.7 | convolution fusion | flops 402710528 | bytes 4194304 | tf_op jit(solution)/shard_map/ps,wsf->wpf/dot_general | solution.py:29
  19.0 2.5 %add_bitcast_fusion = f32[16,64,512]{2,1,0:T(8,128)S(1)} fusion(f32[16,512,64]{1,2,0:T(8,128)S(1)} %fusion.6, f32[16,64,1024]{2,1,0:T(8,128)S(1)} %fusion), kind=kOutput, calls=%fused_computation.6 | convolution fusion | flops 403234816 | bytes 6291456 | tf_op jit(solution)/shard_map/ps,wsf->wpf/dot_general | solution.py:26
  21.6 2.5 %subtract_bitcast_fusion = f32[16,64,512]{2,1,0:T(8,128)S(1)} fusion(f32[16,512,64]{1,2,0:T(8,128)S(1)} %fusion.4, f32[16,64,1024]{2,1,0:T(8,128)S(1)} %fusion), kind=kOutput, calls=%fused_computation.5 | convolution fusion | flops 403234816 | bytes 6291456 | tf_op jit(solution)/shard_map/ps,wsf->wpf/dot_general | solution.py:29
  24.1 2.4 %maximum_multiply_fusion = f32[16,64,1024]{2,1,0:T(8,128)} fusion(f32[16,64,512]{2,1,0:T(8,128)S(1)} %subtract_bitcast_fusion, f32[16,64,512]{2,1,0:T(8,128)S(1)} %add_bitcast_fusion), kind=kLoop, calls=%fused_computation.2 | loop fusion | flops 2097152 | bytes 8388608 | tf_op jit(solution)/shard_map/mul | solution.py:56
  26.5 0.0 copy-start.1
  26.5 0.0 reduce-scatter.3.cloned.1.call-update
  26.5 0.0 reduce-scatter.5.cloned.1.call-start
  26.6 0.6 copy-done.1
  27.2 0.1 eq.47
  27.3 0.0 copy-done
  27.3 0.3 convolution_convert_fusion
  27.5 46.4 %reduce-scatter.3.cloned.1.call-done = f32[256,1024]{1,0:T(8,128)} async-done(((f32[1024,1024]{1,0:T(8,128)}), f32[256,1024]{1,0:T(8,128)}) %reduce-scatter.3.cloned.1.call-update) | async-done | bytes 1048592 | tf_op jit(solution)/shard_map/reduce_scatter | solution.py:55
  73.9 73.1 %all-reduce.1 = bf16[256,1024]{1,0:T(8,128)(2,1)S(1)} all-reduce(f32[256,1024]{1,0:T(8,128)} %reduce-scatter.3.cloned.1.call-done), channel_id=1, replica_groups=mesh['slab'=8,'beam'=4] {'slab'}, use_global_device_ids=true, to_apply=%region_1.2 | all-reduce | flops 262144 | bytes 1572864 | tf_op jit(solution)/shard_map/psum | solution.py:62
  147.0 0.1 slice_negate_fusion
  147.0 0.2 fusion.16
  147.3 0.1 reshape.58
  147.4 0.2 fusion.18
  147.7 0.1 neg.15
  147.8 5.5 %fusion.36 = f32[24,8192]{1,0:T(8,128)} fusion(bf16[512,8192]{1,0:T(8,128)(2,1)} %bitcast.32, bf16[24,256]{1,0:T(8,128)(2,1)S(1)} %neg.15, bf16[24,256]{1,0:T(8,128)(2,1)S(1)} %reshape.58), kind=kOutput, calls=%fused_computation.42 | convolution fusion | flops 201375744 | bytes 9199616 | tf_op jit(solution)/shard_map/dot_general | solution.py:86
  153.3 0.0 reduce-scatter.5.cloned.1.call-update
  153.3 20.4 %reduce-scatter.5.cloned.1.call-done = f32[24,2048]{1,0:T(8,128)} async-done(((f32[24,8192]{1,0:T(8,128)}), f32[24,2048]{1,0:T(8,128)}) %reduce-scatter.5.cloned.1.call-update) | async-done | bytes 196624 | tf_op jit(solution)/shard_map/reduce_scatter | solution.py:87
  (3 shorter events, 0.0 us)
Async XLA Ops:
  6.5 20.7 %copy-start = (bf16[256,1024]{1,0:T(8,128)(2,1)S(1)}, bf16[256,1024]{1,0:T(8,128)(2,1)}, u32[]{:S(2)}) copy-start(bf16[256,1024]{1,0:T(8,128)(2,1)} %param.9) | copy-start | bytes 1572868
  6.5 67.4 %reduce-scatter.3.cloned.1.call-start = ((), (), s32[]{:S(2)}) async-start(), calls=%async_computation.2 | async-start | bytes 5242880 | tf_op jit(solution)/shard_map/reduce_scatter | solution.py:55
  26.5 0.7 copy-start.1
  26.5 147.2 %reduce-scatter.5.cloned.1.call-start = ((), (), s32[]{:S(2)}) async-start(), calls=%async_computation.3 | async-start | bytes 983040 | tf_op jit(solution)/shard_map/reduce_scatter | solution.py:87
Sparse Core Ops, SparseCore 0:
  26.7 47.2 reduce-scatter.2
  153.4 20.2 reduce-scatter.4
where the time goes:
time: 181 us
  blocking collectives  73.1 us (40%)
  waiting for transfers between devices  66.8 us (37%)
  matrix products  22.2 us (12%)
  between operations  13.5 us (7%)
  other arithmetic  3.97 us (2%)
    psum x1, blocking collectives, body(): beam_panel = lax.psum(partial_value, 'slab').astype(jnp.bfloat16)  73.1 us
    reduce_scatter x1, waiting for transfers between devices, body(): lax.psum_scatter(stacked.reshape(WIN_OWN * P_SIZE * lax.axis_size('beam')...  46.4 us
    reduce_scatter x1, waiting for transfers between devices, body(): return lax.psum_scatter(image_part, 'beam', scatter_dimension=1, tiled=True)  20.4 us
    dot_general x1, matrix products, bin_traces(): return jnp.dot(binning, samples, preferred_element_type=jnp.float32)  6.37 us
    dot_general x1, matrix products, body(): jnp.dot(mixture, basis_rows, preferred_element_type=jnp.float32)  5.48 us
  transfers between devices with their start and end apart: 2, of which 2 were waited for; matrix products, arithmetic and copies ran while one was open for 0% of the time, Pallas kernels for 0%

commit v1 on v0

v1 whole, which is shorter than its diff:
```python
import functools

import jax
import jax.numpy as jnp
import numpy as np
from jax import lax
from jax.experimental import pallas as pl
from jax.experimental.pallas import tpu as pltpu
from jax.sharding import PartitionSpec as P

P_SIZE = 64
K = 64
WIN_OWN = 4


def slant_matrix(scale):
    steps = np.arange(K)[:, None] * np.arange(P_SIZE)[None, :] % K
    c = np.cos(2.0 * np.pi * steps / K) * scale
    d = np.sin(2.0 * np.pi * steps / K) * scale
    return np.block([[c, d], [d, -c]]).astype(np.float32)


def wave_kernel(per_step, slabs, window_ref, slot_ref, traces_ref, table_ref, index_ref, out_ref):
    step = pl.program_id(0)

    @pl.when(step == 0)
    def _():
        out_ref[...] = jnp.zeros_like(out_ref)

    traces_per = traces_ref.shape[1]
    half = traces_ref.shape[2] // 2
    rays_n = table_ref.shape[0]
    depths = index_ref.shape[2]
    own = depths // slabs
    ray_rows = lax.broadcasted_iota(jnp.int32, (rays_n, depths), 0)
    slot_rows = lax.broadcasted_iota(jnp.int32, (K, traces_per), 0)
    for t in range(per_step):
        w = window_ref[step * per_step + t]
        pick = (ray_rows == index_ref[w]).astype(jnp.float32).astype(jnp.bfloat16)
        rays = lax.dot_general(
            pick, table_ref[...], (((0,), (0,)), ((), ())), preferred_element_type=jnp.float32
        ).astype(jnp.bfloat16)
        bins = (slot_rows == slot_ref[t]).astype(jnp.float32).astype(jnp.bfloat16)
        binned = jnp.dot(bins, traces_ref[t], preferred_element_type=jnp.float32)
        re, im = binned[:, :half], binned[:, half:]
        both = jnp.concatenate(
            [jnp.concatenate([re, -im], axis=1), jnp.concatenate([im, re], axis=1)], axis=0
        )
        high = both.astype(jnp.bfloat16)
        low = (both - high.astype(jnp.float32)).astype(jnp.bfloat16)
        parts = lax.dot_general(
            rays,
            jnp.concatenate([high, low], axis=0),
            (((1,), (1,)), ((), ())),
            preferred_element_type=jnp.float32,
        )
        part = parts[:, : 2 * K] + parts[:, 2 * K :]
        for s in range(slabs):
            out_ref[s, w] += part[s * own : (s + 1) * own]


def local_waves(traces, shot_window, trace_slot, ray_phase, index_all, slabs):
    shots, per_shot, doubled = traces.shape
    windows, depths = index_all.shape
    per_step = 4 if shots % 4 == 0 else 1
    grid_spec = pltpu.PrefetchScalarGridSpec(
        num_scalar_prefetch=1,
        grid=(shots // per_step,),
        in_specs=[
            pl.BlockSpec((per_step, 1, per_shot), lambda i, w: (i, 0, 0)),
            pl.BlockSpec((per_step, per_shot, doubled), lambda i, w: (i, 0, 0)),
            pl.BlockSpec(ray_phase.shape, lambda i, w: (0, 0)),
            pl.BlockSpec((windows, 1, depths), lambda i, w: (0, 0, 0)),
        ],
        out_specs=pl.BlockSpec((slabs, windows, depths // slabs, 2 * K), lambda i, w: (0, 0, 0, 0)),
    )
    return pl.pallas_call(
        functools.partial(wave_kernel, per_step, slabs),
        out_shape=jax.ShapeDtypeStruct((slabs, windows, depths // slabs, 2 * K), jnp.float32),
        grid_spec=grid_spec,
        compiler_params=pltpu.CompilerParams(vmem_limit_bytes=40 * 1024 * 1024),
        name="local_waves",
    )(
        shot_window,
        trace_slot.reshape(shots, 1, per_shot),
        traces,
        ray_phase,
        index_all.reshape(windows, 1, depths),
    )


def body(traces, shot_window, trace_slot, ray_phase, ray_index, beam_basis):
    shots, per_shot, doubled = traces.shape
    beams = lax.axis_size("beam")
    slabs = lax.axis_size("slab")
    scale = (shots * slabs * beams * per_shot / (WIN_OWN * beams)) ** (-0.5)
    depths = ray_index.shape[1]
    index_all = lax.all_gather(ray_index, ("slab", "beam"))
    index_all = (
        index_all.reshape(slabs, beams, WIN_OWN, depths)
        .transpose(1, 2, 0, 3)
        .reshape(beams * WIN_OWN, slabs * depths)
    )
    waves = local_waves(traces, shot_window, trace_slot, ray_phase, index_all, slabs)
    waves = waves.reshape(slabs, beams, WIN_OWN * depths, 2 * K)
    waves = lax.psum_scatter(waves, "beam", scatter_dimension=1, tiled=False)
    waves = lax.psum_scatter(waves, "slab", scatter_dimension=0, tiled=False)
    wave = jnp.dot(waves, slant_matrix(scale), precision=lax.Precision.HIGHEST)
    wave = wave.reshape(WIN_OWN, depths, 2, P_SIZE).transpose(1, 2, 0, 3)
    mixture = wave.reshape(depths, 2 * WIN_OWN * P_SIZE)
    high = mixture.astype(jnp.bfloat16)
    low = (mixture - high.astype(jnp.float32)).astype(jnp.bfloat16)
    basis_rows = beam_basis.reshape(2 * WIN_OWN * P_SIZE, beam_basis.shape[2])
    both = jnp.dot(
        jnp.concatenate([high, low], axis=0), basis_rows, preferred_element_type=jnp.float32
    )
    image_part = both[:depths] + both[depths:]
    return lax.psum_scatter(image_part, "beam", scatter_dimension=1, tiled=True)


def solution(mesh):
    in_specs = (
        P(("slab", "beam"), None, None),
        P(("slab", "beam")),
        P(("slab", "beam"), None),
        P(),
        P("beam", "slab"),
        P(None, "beam", None),
    )
    out_specs = P("slab", "beam")
    return jax.shard_map(body, mesh=mesh, in_specs=in_specs, out_specs=out_specs, check_vma=False)
```

time: 181 us -> 204 us (1.13)
  waiting for transfers between devices: 66.8 us -> 123 us
  blocking collectives: 73.1 us -> 43.6 us
  matrix products: 22.2 us -> 6.08 us
  Pallas kernels: 0 us -> 8.97 us
  local copies, waits for them, and re-layouts: 0.92 us -> 8.44 us
  other arithmetic: 3.97 us -> 0.97 us
    psum x1 -> x0, blocking collectives: 73.1 us -> none  [body(): beam_panel = lax.psum(partial_value, 'slab').astype(jnp.bfloat16)]
    all_gather x0 -> x1, blocking collectives: none -> 43.6 us  [body(): index_all = lax.all_gather(ray_index, ('slab', 'beam'))]
    unnamed x2 -> x4, waiting for transfers between devices: 0.03 us -> 38 us
    dot_general x9 -> x2, matrix products: 22.2 us -> 6.08 us  [the longest x1 4.95 us: body(): jnp.dot(jnp.concatenate([high, low], axis=0), basis_rows, preferred_eleme...]
    reduce_scatter x1, waiting for transfers between devices: 46.4 us -> 62.2 us  [body(): waves = lax.psum_scatter(waves, 'slab', scatter_dimension=0, tiled=False)]
    pallas_call x0 -> x1, Pallas kernels: none -> 8.97 us  [local_waves(): pl.pallas_call(functools.partial(wave_kernel, per_step, slabs), out_shape...]
    unnamed x4 -> x13, local copies, waits for them, and re-layouts: 0.61 us -> 5.74 us
    mul x2 -> x0, other arithmetic: 3.15 us -> none  [the longest x1 2.43 us: body(): stacked.reshape(WIN_OWN * P_SIZE * lax.axis_size('beam'), doubled)]
  transfers between devices with their start and end apart: 2 -> 3, of which waited for: 2 -> 3; matrix products, arithmetic and copies ran while one was open for 0% -> 0% of each run, Pallas kernels for 0% -> 0%
where the time goes in v1:
time: 204 us
  waiting for transfers between devices  123 us (60%)
  blocking collectives  43.6 us (21%)
  between operations  13.2 us (6%)
  Pallas kernels  8.97 us (4%)
  local copies, waits for them, and re-layouts  8.44 us (4%)
  matrix products  6.08 us (3%)
    reduce_scatter x1, waiting for transfers between devices, body(): waves = lax.psum_scatter(waves, 'slab', scatter_dimension=0, tiled=False)  62.2 us
    all_gather x1, blocking collectives, body(): index_all = lax.all_gather(ray_index, ('slab', 'beam'))  43.6 us
    unnamed x4, waiting for transfers between devices  38 us
    reduce_scatter x1, waiting for transfers between devices, body(): return lax.psum_scatter(image_part, 'beam', scatter_dimension=1, tiled=True)  22.5 us
    pallas_call x1, Pallas kernels, local_waves(): pl.pallas_call(functools.partial(wave_kernel, per_step, slabs), out_shape...  8.97 us
    unnamed x13, local copies, waits for them, and re-layouts  5.74 us
    dot_general x1, matrix products, body(): jnp.dot(jnp.concatenate([high, low], axis=0), basis_rows, preferred_eleme...  4.95 us
  transfers between devices with their start and end apart: 3, of which 3 were waited for; matrix products, arithmetic and copies ran while one was open for 0% of the time, Pallas kernels for 0%

profile of v1, /device:TPU:0, one launch (start us, length us, event | category | flops | bytes accessed | tf_op | source)
XLA Modules:
  0.0 203.9 jit_solution(14301476997063378627)
XLA Ops:
  6.5 0.0 all-reduce.3.cloned.1.call-start
  6.5 43.6 %all-gather.1 = s32[32,4,24]{2,1,0:T(4,128)S(1)} all-gather(s32[1,4,24]{2,1,0:T(4,128)} %bitcast.35), channel_id=2, replica_groups=mesh['slab'=8,'beam'=4] {'slab','beam'}, dimensions={0}, use_global_device_ids=true | all-gather | bytes 12672 | tf_op jit(solution)/shard_map/all_gather | solution.py:98
  50.2 0.1 reshape_reshape.3.index_ref
  50.3 0.0 copy-start
  50.3 2.2 %copy-done = bf16[16,128,1024]{2,1,0:T(8,128)(2,1)S(1)} copy-done((bf16[16,128,1024]{2,1,0:T(8,128)(2,1)S(1)}, bf16[16,128,1024]{2,1,0:T(8,128)(2,1)}, u32[]{:S(2)}) %copy-start) | copy-done | bytes 4194328
  52.5 0.0 copy-start.1
  52.5 1.0 copy-done.1
  53.5 0.0 copy-start.2
  53.5 0.7 copy-done.2
  54.2 0.0 copy-start.3
  54.2 0.7 copy-done.3
  54.9 9.0 %local_waves.1 = f32[8,16,24,128]{3,2,1,0:T(8,128)} custom-call(s32[16]{0:T(128)S(1)} %copy-done.3, s32[16,1,128]{2,1,0:T(1,128)S(1)} %bitcast.30, bf16[16,128,1024]{2,1,0:T(8,128)(2,1)S(1)} %copy-done, bf16[256,1024]{1,0:T(8,128)(2,1)S(1)} %copy-done.1, s32[16,1,192]{2,1,0:T(1,128)S(1)} %reshape_reshape.3.index_ref), custom_call_target="tpu_custom_call" | custom-call | tf_op jit(solution)/shard_map/local_waves/pallas_call | solution.py:77
  63.8 0.0 copy-start.5
  63.8 0.0 copy-start.4
  63.8 0.0 all-reduce.3.cloned.1.call-update
  63.9 0.0 reduce-scatter.6.cloned.1.call-start
  63.9 0.6 copy-done.5
  64.5 0.6 dynamic-slice
  65.1 37.9 %all-reduce.3.cloned.1.call-done = f32[8,4,96,128]{3,2,1,0:T(8,128)} async-done(((f32[8,4,96,128]{3,2,1,0:T(8,128)}), f32[8,4,96,128]{3,2,1,0:T(8,128)}) %all-reduce.3.cloned.1.call-update) | async-done | bytes 1572880
  103.0 2.4 %dynamic-slice_bitcast_fusion = f32[8,96,128]{2,1,0:T(8,128)} fusion(f32[8,4,96,128]{3,2,1,0:T(8,128)} %all-reduce.3.cloned.1.call-done, u32[]{:T(128)} %bitcast.18), kind=kLoop, calls=%fused_computation.2 | loop fusion | bytes 786436 | tf_op jit(solution)/shard_map/reduce_scatter | solution.py:106
  105.4 0.0 reduce-scatter.6.cloned.1.call-update
  105.4 0.0 reduce-scatter.8.cloned.1.call-start
  105.5 62.2 %reduce-scatter.6.cloned.1.call-done = f32[1,96,128]{2,1,0:T(8,128)} async-done(((f32[8,96,128]{2,1,0:T(8,128)}), f32[1,96,128]{2,1,0:T(8,128)}) %reduce-scatter.6.cloned.1.call-update) | async-done | bytes 49168 | tf_op jit(solution)/shard_map/reduce_scatter | solution.py:107
  167.7 0.0 copy-done.4
  167.7 1.1 convolution_bitcast_fusion
  168.9 0.1 reshape.22
  169.0 5.0 %fusion = f32[48,8192]{1,0:T(8,128)S(1)} fusion(bf16[512,8192]{1,0:T(8,128)(2,1)} %bitcast.31, bf16[24,512]{1,0:T(8,128)(2,1)S(1)} %get-tuple-element.5, bf16[24,512]{1,0:T(8,128)(2,1)S(1)} %get-tuple-element.6), kind=kOutput, calls=%fused_computation.4 | convolution fusion | flops 402751488 | bytes 10010624 | tf_op jit(solution)/shard_map/dot_general | solution.py:114
  173.9 1.0 slice_add_fusion
  174.9 0.0 reduce-scatter.8.cloned.1.call-update
  174.9 22.5 %reduce-scatter.8.cloned.1.call-done = f32[24,2048]{1,0:T(8,128)} async-done(((f32[24,8192]{1,0:T(8,128)}), f32[24,2048]{1,0:T(8,128)}) %reduce-scatter.8.cloned.1.call-update) | async-done | bytes 196624 | tf_op jit(solution)/shard_map/reduce_scatter | solution.py:118
  (3 shorter events, 0.1 us)
Async XLA Ops:
  6.5 96.5 %all-reduce.3.cloned.1.call-start = ((), (), s32[]{:S(2)}) async-start(), calls=%async_computation.4 | async-start | bytes 3145728
  50.3 2.2 %copy-start = (bf16[16,128,1024]{2,1,0:T(8,128)(2,1)S(1)}, bf16[16,128,1024]{2,1,0:T(8,128)(2,1)}, u32[]{:S(2)}) copy-start(bf16[16,128,1024]{2,1,0:T(8,128)(2,1)} %traces_ref.1) | copy-start | bytes 12582916
  52.5 1.0 copy-start.1
  53.5 0.7 copy-start.2
  54.2 0.7 copy-start.3
  63.8 0.7 copy-start.5
  63.8 103.8 %copy-start.4 = (f32[2,64,128,1]{2,1,0,3:T(8,128)S(1)}, f32[2,64,128,1]{2,1,0,3:T(8,128)}, u32[]{:S(2)}) copy-start(f32[2,64,128,1]{2,1,0,3:T(8,128)} %constant.12) | copy-start | bytes 196612
  63.9 103.8 %reduce-scatter.6.cloned.1.call-start = ((), (), s32[]{:S(2)}) async-start(), calls=%async_computation.2 | async-start | bytes 442368 | tf_op jit(solution)/shard_map/reduce_scatter | solution.py:107
  105.4 91.9 %reduce-scatter.8.cloned.1.call-start = ((), (), s32[]{:S(2)}) async-start(), calls=%async_computation.3 | async-start | bytes 983040 | tf_op jit(solution)/shard_map/reduce_scatter | solution.py:118
Sparse Core Ops, SparseCore 0:
  64.0 38.9 all-reduce.2
  106.3 61.3 reduce-scatter.5
  175.1 22.2 reduce-scatter.7

commit v2 on v1

--- a/solution.py
+++ b/solution.py
@@ -11,6 +11,9 @@
 P_SIZE = 64
 K = 64
 WIN_OWN = 4
+MESH = pl.DeviceIdType.MESH
+F32 = jnp.float32
+BF16 = jnp.bfloat16
 
 
 def slant_matrix(scale):
@@ -32,10 +35,13 @@
     rays_n = table_ref.shape[0]
     depths = index_ref.shape[2]
     own = depths // slabs
+    windows = index_ref.shape[0]
     ray_rows = lax.broadcasted_iota(jnp.int32, (rays_n, depths), 0)
     slot_rows = lax.broadcasted_iota(jnp.int32, (K, traces_per), 0)
     for t in range(per_step):
         w = window_ref[step * per_step + t]
+        owner, own_w = w // WIN_OWN, w % WIN_OWN
+        place = ((owner % 2) * (windows // (2 * WIN_OWN)) + owner // 2) * WIN_OWN + own_w
         pick = (ray_rows == index_ref[w]).astype(jnp.float32).astype(jnp.bfloat16)
         rays = lax.dot_general(
             pick, table_ref[...], (((0,), (0,)), ((), ())), preferred_element_type=jnp.float32
@@ -56,7 +62,7 @@
         )
         part = parts[:, : 2 * K] + parts[:, 2 * K :]
         for s in range(slabs):
-            out_ref[s, w] += part[s * own : (s + 1) * own]
+            out_ref[s, place] += part[s * own : (s + 1) * own]
 
 
 def local_waves(traces, shot_window, trace_slot, ray_phase, index_all, slabs):
@@ -89,33 +95,243 @@
     )
 
 
+def gather_kernel(slabs, beams, mine_ref, out_ref, held, beam_send, beam_recv, slab_send, slab_recv):
+    slab, beam = lax.axis_index("slab"), lax.axis_index("beam")
+    beam_peers = [lax.rem(beam + j, beams) for j in range(1, beams)]
+    slab_peers = [lax.rem(slab + k, slabs) for k in range(1, slabs)]
+    barrier = pltpu.get_barrier_semaphore()
+    for b in beam_peers:
+        pl.semaphore_signal(barrier, inc=1, device_id=(slab, b), device_id_type=MESH)
+    for s in slab_peers:
+        pl.semaphore_signal(barrier, inc=1, device_id=(s, beam), device_id_type=MESH)
+    held[0, 0] = mine_ref[...]
+    pl.semaphore_wait(barrier, beams + slabs - 2)
+    copies = []
+    for j, b in enumerate(beam_peers):
+        copy = pltpu.make_async_remote_copy(
+            src_ref=held.at[0, 0],
+            dst_ref=held.at[0, j + 1],
+            send_sem=beam_send.at[j],
+            recv_sem=beam_recv.at[j],
+            device_id=(slab, b),
+            device_id_type=MESH,
+        )
+        copy.start()
+        copies.append(copy)
+    for copy in copies:
+        copy.wait()
+    copies = []
+    for k, s in enumerate(slab_peers):
+        copy = pltpu.make_async_remote_copy(
+            src_ref=held.at[0],
+            dst_ref=held.at[k + 1],
+            send_sem=slab_send.at[k],
+            recv_sem=slab_recv.at[k],
+            device_id=(s, beam),
+            device_id_type=MESH,
+        )
+        copy.start()
+        copies.append(copy)
+    for copy in copies:
+        copy.wait()
+    for k in range(slabs):
+        for j in range(beams):
+            s = lax.rem(slab + slabs - k, slabs)
+            b = lax.rem(beam + beams - j, beams)
+            out_ref[s, b] = held[k, j]
+
+
+def gather_index(ray_index, slabs, beams):
+    rows, depths = ray_index.shape
+    block = (-(-rows // 8) * 8, -(-depths // 128) * 128)
+    mine = jnp.pad(ray_index, ((0, block[0] - rows), (0, block[1] - depths)))
+    vmem = pl.BlockSpec(memory_space=pltpu.VMEM)
+    out = pl.pallas_call(
+        functools.partial(gather_kernel, slabs, beams),
+        out_shape=jax.ShapeDtypeStruct((slabs, beams) + block, jnp.int32),
+        in_specs=[vmem],
+        out_specs=vmem,
+        scratch_shapes=[
+            pltpu.VMEM((slabs, beams) + block, jnp.int32),
+            pltpu.SemaphoreType.DMA((beams,)),
+            pltpu.SemaphoreType.DMA((beams,)),
+            pltpu.SemaphoreType.DMA((slabs,)),
+            pltpu.SemaphoreType.DMA((slabs,)),
+        ],
+        compiler_params=pltpu.CompilerParams(collective_id=0, has_side_effects=True),
+        name="gather_index",
+    )(mine)
+    out = out[:, :, :rows, :depths].transpose(1, 2, 0, 3)
+    return out.reshape(beams * rows, slabs * depths)
+
+
+def image_kernel(
+    slabs, chips, waves, slant, basis_hbm, out_ref,
+    basis, core_in, chip_out, chip_in, slab_out, slab_in, part_out, part_in, edge_out, edge_in,
+    basis_sem, core_s, core_r, chip_s, chip_r, slab_s, slab_r, part_s, part_r, edge_s, edge_r,
+):
+    slab, beam = lax.axis_index("slab"), lax.axis_index("beam")
+    core, chip = lax.rem(beam, 2), lax.div(beam, 2)
+    other = 1 - core
+    sibling = (slab, 2 * chip + other)
+    chip_of = [lax.rem(chip + j, chips) for j in range(chips)]
+    slab_of = [lax.rem(slab + k, slabs) for k in range(1, slabs)] + [slab]
+
+    load = pltpu.make_async_copy(basis_hbm, basis, basis_sem)
+    load.start()
+    barrier = pltpu.get_barrier_semaphore()
+    peers = [sibling]
+    peers += [(slab, 2 * x + core) for x in chip_of[1:]]
+    peers += [(s, beam) for s in slab_of[:-1]]
+    for peer in peers:
+        pl.semaphore_signal(barrier, inc=1, device_id=peer, device_id_type=MESH)
+    pl.semaphore_wait(barrier, len(peers))
+
+    def send(src, dst, send_sem, recv_sem, device):
+        copy = pltpu.make_async_remote_copy(
+            src_ref=src, dst_ref=dst, send_sem=send_sem, recv_sem=recv_sem,
+            device_id=device, device_id_type=MESH,
+        )
+        copy.start()
+        return copy
+
+    sent = []
+    core_copies = [
+        send(waves.at[s, other], core_in.at[k], core_s.at[k], core_r.at[k], sibling)
+        for k, s in enumerate(slab_of)
+    ]
+    chip_copies = []
+    for k, s in enumerate(slab_of):
+        core_copies[k].wait_recv()
+        row = []
+        for j in range(1, chips):
+            x = chip_of[j]
+            chip_out[k, j - 1] = (waves[s, core, x] + core_in[k, x]).astype(BF16)
+            row.append(
+                send(
+                    chip_out.at[k, j - 1], chip_in.at[k, j - 1],
+                    chip_s.at[k, j - 1], chip_r.at[k, j - 1], (slab, 2 * x + core),
+                )
+            )
+        chip_copies.append(row)
+    slab_copies = []
+    total = None
+    for k, s in enumerate(slab_of):
+        total = waves[s, core, chip] + core_in[k, chip]
+        for j, copy in enumerate(chip_copies[k]):
+            copy.wait_recv()
+            total = total + chip_in[k, j].astype(F32)
+        if k < slabs - 1:
+            slab_out[k] = total.astype(BF16)
+            slab_copies.append(
+                send(slab_out.at[k], slab_in.at[k], slab_s.at[k], slab_r.at[k], (s, beam))
+            )
+    for k, copy in enumerate(slab_copies):
+        copy.wait_recv()
+        total = total + slab_in[k].astype(F32)
+    wave = jnp.dot(
+        total, slant[...], precision=lax.Precision.HIGHEST, preferred_element_type=F32
+    )
+    depths = out_ref.shape[0]
+    lateral = out_ref.shape[1]
+    rows = [wave[w * depths : (w + 1) * depths] for w in range(WIN_OWN)]
+    mixed = []
+    for lo in (0, P_SIZE):
+        part = jnp.concatenate([r[:, lo : lo + P_SIZE] for r in rows], axis=1)
+        high = part.astype(BF16)
+        low = (part - high.astype(F32))
+        mixed.append(jnp.concatenate([high.astype(F32), low], axis=0).astype(BF16))
+    load.wait()
+
+    def terms(owner):
+        cols = pl.ds(pl.multiple_of(owner * lateral, lateral), lateral)
+        both = jnp.dot(mixed[0], basis[0, :, cols], preferred_element_type=F32)
+        both += jnp.dot(mixed[1], basis[1, :, cols], preferred_element_type=F32)
+        return both[:depths] + both[depths:]
+
+    order = list(range(1, chips)) + [0]
+    part_copies = {}
+    for j in order:
+        part_out[j] = terms(2 * chip_of[j] + other)
+        part_copies[j] = send(
+            part_out.at[j], part_in.at[j], part_s.at[j], part_r.at[j], sibling
+        )
+    edge_copies = []
+    half = lateral // 2
+    for j in range(1, chips):
+        value = terms(2 * chip_of[j] + core)
+        part_copies[j].wait_recv()
+        value = value + part_in[j]
+        edge_out[j - 1] = jnp.concatenate([value[:, :half], value[:, half:]], axis=0).astype(BF16)
+        edge_copies.append(
+            send(
+                edge_out.at[j - 1], edge_in.at[j - 1], edge_s.at[j - 1], edge_r.at[j - 1],
+                (slab, 2 * chip_of[j] + core),
+            )
+        )
+    value = terms(beam)
+    part_copies[0].wait_recv()
+    out_ref[...] = value + part_in[0]
+    for j, copy in enumerate(edge_copies):
+        copy.wait_recv()
+        edge = edge_in[j].astype(F32)
+        out_ref[:, :half] += edge[:depths]
+        out_ref[:, half:] += edge[depths:]
+    sent = core_copies + slab_copies + list(part_copies.values()) + edge_copies
+    for row in chip_copies:
+        sent += row
+    for copy in sent:
+        copy.wait_send()
+
+
+def sum_and_image(waves, slant, basis, slabs, beams, depths):
+    chips = beams // 2
+    lateral = basis.shape[2] // beams
+    rows = waves.shape[3]
+    wide = 2 * K
+    hops = max(chips - 1, 1)
+    vmem = pl.BlockSpec(memory_space=pltpu.VMEM)
+    dma = pltpu.SemaphoreType.DMA
+    return pl.pallas_call(
+        functools.partial(image_kernel, slabs, chips),
+        out_shape=jax.ShapeDtypeStruct((depths, lateral), F32),
+        in_specs=[vmem, vmem, pl.BlockSpec(memory_space=pl.ANY)],
+        out_specs=vmem,
+        scratch_shapes=[
+            pltpu.VMEM(basis.shape, BF16),
+            pltpu.VMEM((slabs, chips, rows, wide), F32),
+            pltpu.VMEM((slabs, hops, rows, wide), BF16),
+            pltpu.VMEM((slabs, hops, rows, wide), BF16),
+            pltpu.VMEM((slabs, rows, wide), BF16),
+            pltpu.VMEM((slabs, rows, wide), BF16),
+            pltpu.VMEM((chips, depths, lateral), F32),
+            pltpu.VMEM((chips, depths, lateral), F32),
+            pltpu.VMEM((hops, 2 * depths, lateral // 2), BF16),
+            pltpu.VMEM((hops, 2 * depths, lateral // 2), BF16),
+            dma(()),
+            dma((slabs,)), dma((slabs,)),
+            dma((slabs, hops)), dma((slabs, hops)),
+            dma((slabs,)), dma((slabs,)),
+            dma((chips,)), dma((chips,)),
+            dma((hops,)), dma((hops,)),
+        ],
+        compiler_params=pltpu.CompilerParams(
+            collective_id=1, has_side_effects=True, vmem_limit_bytes=48 * 1024 * 1024
+        ),
+        name="sum_and_image",
+    )(waves, slant, basis)
+
+
 def body(traces, shot_window, trace_slot, ray_phase, ray_index, beam_basis):
     shots, per_shot, doubled = traces.shape
     beams = lax.axis_size("beam")
     slabs = lax.axis_size("slab")
     scale = (shots * slabs * beams * per_shot / (WIN_OWN * beams)) ** (-0.5)
     depths = ray_index.shape[1]
-    index_all = lax.all_gather(ray_index, ("slab", "beam"))
-    index_all = (
-        index_all.reshape(slabs, beams, WIN_OWN, depths)
-        .transpose(1, 2, 0, 3)
-        .reshape(beams * WIN_OWN, slabs * depths)
-    )
+    index_all = gather_index(ray_index, slabs, beams)
     waves = local_waves(traces, shot_window, trace_slot, ray_phase, index_all, slabs)
-    waves = waves.reshape(slabs, beams, WIN_OWN * depths, 2 * K)
-    waves = lax.psum_scatter(waves, "beam", scatter_dimension=1, tiled=False)
-    waves = lax.psum_scatter(waves, "slab", scatter_dimension=0, tiled=False)
-    wave = jnp.dot(waves, slant_matrix(scale), precision=lax.Precision.HIGHEST)
-    wave = wave.reshape(WIN_OWN, depths, 2, P_SIZE).transpose(1, 2, 0, 3)
-    mixture = wave.reshape(depths, 2 * WIN_OWN * P_SIZE)
-    high = mixture.astype(jnp.bfloat16)
-    low = (mixture - high.astype(jnp.float32)).astype(jnp.bfloat16)
-    basis_rows = beam_basis.reshape(2 * WIN_OWN * P_SIZE, beam_basis.shape[2])
-    both = jnp.dot(
-        jnp.concatenate([high, low], axis=0), basis_rows, preferred_element_type=jnp.float32
-    )
-    image_part = both[:depths] + both[depths:]
-    return lax.psum_scatter(image_part, "beam", scatter_dimension=1, tiled=True)
+    waves = waves.reshape(slabs, 2, beams // 2, WIN_OWN * depths, 2 * K)
+    return sum_and_image(waves, slant_matrix(scale), beam_basis, slabs, beams, depths)
 
 
 def solution(mesh):

time: 204 us -> 49.8 us (0.24)
  waiting for transfers between devices: 123 us -> 0 us
  blocking collectives: 43.6 us -> 0 us
  Pallas kernels: 8.97 us -> 41.8 us
  between operations: 13.2 us -> 0.06 us
  matrix products: 6.08 us -> 0 us
    reduce_scatter x2 -> x0, waiting for transfers between devices: 84.6 us -> none  [the longest x1 62.2 us: body(): waves = lax.psum_scatter(waves, 'slab', scatter_dimension=0, tiled=False)]
    all_gather x1 -> x0, blocking collectives: 43.6 us -> none  [body(): index_all = lax.all_gather(ray_index, ('slab', 'beam'))]
    unnamed x4 -> x0, waiting for transfers between devices: 38 us -> none
    pallas_call x0 -> x2, Pallas kernels: none -> 34 us  [the longest x1 20 us: sum_and_image(): pl.pallas_call(functools.partial(image_kernel, slabs, chips), out_shape=j...]
    dot_general x2 -> x0, matrix products: 6.08 us -> none  [the longest x1 4.95 us: body(): jnp.dot(jnp.concatenate([high, low], axis=0), basis_rows, preferred_eleme...]
    reduce_scatter x1 -> x0, local copies, waits for them, and re-layouts: 2.43 us -> none  [body(): waves = lax.psum_scatter(waves, 'beam', scatter_dimension=1, tiled=False)]
    unnamed x13 -> x11, local copies, waits for them, and re-layouts: 5.74 us -> 5.26 us
  transfers between devices with their start and end apart: 3 -> 0, of which waited for: 3 -> 0; matrix products, arithmetic and copies ran while one was open for 0% -> 0% of each run, Pallas kernels for 0% -> 0%
where the time goes in v2:
time: 49.8 us; the launch traced here: 49.5 us
  Pallas kernels  41.8 us (84%)
  local copies, waits for them, and re-layouts  7.61 us (15%)
    pallas_call x1, Pallas kernels, sum_and_image(): pl.pallas_call(functools.partial(image_kernel, slabs, chips), out_shape=j...  20 us
    pallas_call x1, Pallas kernels, gather_index(): pl.pallas_call(functools.partial(gather_kernel, slabs, beams), out_shape=...  14 us
    pallas_call x1, Pallas kernels, local_waves(): pl.pallas_call(functools.partial(wave_kernel, per_step, slabs), out_shape...  7.82 us
    unnamed x11, local copies, waits for them, and re-layouts  5.26 us
    pad x1, local copies, waits for them, and re-layouts, gather_index(): mine = jnp.pad(ray_index, ((0, block[0] - rows), (0, block[1] - depths)))  1.31 us

profile of v2, /device:TPU:0, one launch (start us, length us, event | category | flops | bytes accessed | tf_op | source)
XLA Modules:
  0.0 49.5 jit_solution(10533496780722831545)
XLA Ops:
  0.0 0.0 copy-start.2
  0.0 1.3 %pad.4.mine_ref = s32[8,128]{1,0:T(8,128)} pad(s32[4,24]{1,0:T(4,128)} %param.11, s32[]{:T(128)} %constant.1.clone.1), padding=0_4x0_104 | pad | bytes 4484 | tf_op jit(solution)/shard_map/jit(_pad)/pad | solution.py:147
  1.3 14.0 %gather_index.1 = s32[8,4,8,128]{3,2,1,0:T(8,128)} custom-call(s32[8,128]{1,0:T(8,128)} %pad.4.mine_ref), custom_call_target="tpu_custom_call" | custom-call | tf_op jit(solution)/shard_map/gather_index/pallas_call | solution.py:149
  15.3 0.9 %slice_bitcast_fusion = s32[4,4,8,24]{3,1,0,2:T(4,128)S(1)} fusion(s32[8,4,8,128]{3,2,1,0:T(8,128)} %gather_index.1), kind=kLoop, calls=%fused_computation | loop fusion | bytes 24576 | tf_op jit(solution)/shard_map/transpose | solution.py:164
  16.3 0.1 reshape_reshape.3.index_ref
  16.4 0.0 copy-start
  16.4 2.2 %copy-done = bf16[16,128,1024]{2,1,0:T(8,128)(2,1)S(1)} copy-done((bf16[16,128,1024]{2,1,0:T(8,128)(2,1)S(1)}, bf16[16,128,1024]{2,1,0:T(8,128)(2,1)}, u32[]{:S(2)}) %copy-start) | copy-done | bytes 4194328
  18.6 0.0 copy-start.1
  18.6 1.0 %copy-done.1 = bf16[256,1024]{1,0:T(8,128)(2,1)S(1)} copy-done((bf16[256,1024]{1,0:T(8,128)(2,1)S(1)}, bf16[256,1024]{1,0:T(8,128)(2,1)}, u32[]{:S(2)}) %copy-start.1) | copy-done | bytes 524312
  19.6 0.0 copy-start.3
  19.6 0.7 %copy-done.3 = s32[16,128]{1,0:T(8,128)S(1)} copy-done((s32[16,128]{1,0:T(8,128)S(1)}, s32[16,128]{1,0:T(8,128)}, u32[]{:S(2)}) %copy-start.3) | copy-done | bytes 8216
  20.3 0.0 copy-start.4
  20.3 0.7 %copy-done.4 = s32[16]{0:T(128)S(1)} copy-done((s32[16]{0:T(128)S(1)}, s32[16]{0:T(128)}, u32[]{:S(2)}) %copy-start.4) | copy-done | bytes 88
  21.0 7.8 %local_waves.1 = f32[8,16,24,128]{3,2,1,0:T(8,128)S(1)} custom-call(s32[16]{0:T(128)S(1)} %copy-done.4, s32[16,1,128]{2,1,0:T(1,128)S(1)} %bitcast.7, bf16[16,128,1024]{2,1,0:T(8,128)(2,1)S(1)} %copy-done, bf16[256,1024]{1,0:T(8,128)(2,1)S(1)} %copy-done.1, s32[16,1,192]{2,1,0:T(1,128)S(1)} %reshape_reshape.3.index_ref), custom_call_target="tpu_custom_call" | custom-call | tf_op jit(solution)/shard_map/local_waves/pallas_call | solution.py:83
  28.8 0.0 copy-done.2
  28.8 20.0 %sum_and_image.1 = f32[24,2048]{1,0:T(8,128)S(1)} custom-call(f32[8,2,2,96,128]{4,3,2,1,0:T(8,128)S(1)} %bitcast.6, f32[128,128]{1,0:T(8,128)S(1)} %copy-done.2, bf16[2,256,8192]{2,1,0:T(8,128)(2,1)} %basis_hbm.1), custom_call_target="tpu_custom_call" | custom-call | tf_op jit(solution)/shard_map/sum_and_image/pallas_call | solution.py:295
  48.8 0.7 %copy.10 = f32[24,2048]{1,0:T(8,128)} copy(f32[24,2048]{1,0:T(8,128)S(1)} %sum_and_image.1) | data formatting | bytes 393216
  (1 shorter events, 0.0 us)
Async XLA Ops:
  0.0 28.8 %copy-start.2 = (f32[128,128]{1,0:T(8,128)S(1)}, f32[128,128]{1,0:T(8,128)}, u32[]{:S(2)}) copy-start(f32[128,128]{1,0:T(8,128)} %constant.4.clone.slant) | copy-start | bytes 196612
  16.4 2.2 %copy-start = (bf16[16,128,1024]{2,1,0:T(8,128)(2,1)S(1)}, bf16[16,128,1024]{2,1,0:T(8,128)(2,1)}, u32[]{:S(2)}) copy-start(bf16[16,128,1024]{2,1,0:T(8,128)(2,1)} %traces_ref.1) | copy-start | bytes 12582916
  18.6 1.0 %copy-start.1 = (bf16[256,1024]{1,0:T(8,128)(2,1)S(1)}, bf16[256,1024]{1,0:T(8,128)(2,1)}, u32[]{:S(2)}) copy-start(bf16[256,1024]{1,0:T(8,128)(2,1)} %table_ref.1) | copy-start | bytes 1572868
  19.6 0.7 %copy-start.3 = (s32[16,128]{1,0:T(8,128)S(1)}, s32[16,128]{1,0:T(8,128)}, u32[]{:S(2)}) copy-start(s32[16,128]{1,0:T(8,128)} %param.9) | copy-start | bytes 24580
  20.3 0.7 %copy-start.4 = (s32[16]{0:T(128)S(1)}, s32[16]{0:T(128)}, u32[]{:S(2)}) copy-start(s32[16]{0:T(128)} %window_ref.1) | copy-start | bytes 196

commit v3 on v2

v3 whole, which is shorter than its diff:
```python
import functools

import jax
import jax.numpy as jnp
import numpy as np
from jax import lax
from jax.experimental import pallas as pl
from jax.experimental.pallas import tpu as pltpu
from jax.sharding import PartitionSpec as P

P_SIZE = 64
K = 64
WIN_OWN = 4
MESH = pl.DeviceIdType.MESH
F32 = jnp.float32
BF16 = jnp.bfloat16


def slant_matrix(scale):
    steps = np.arange(K)[:, None] * np.arange(P_SIZE)[None, :] % K
    c = np.cos(2.0 * np.pi * steps / K) * scale
    d = np.sin(2.0 * np.pi * steps / K) * scale
    return np.block([[c, d], [d, -c]]).astype(np.float32)


def migrate_kernel(
    slabs, beams, window_ref, slot_ref, index_ref, slant, traces_hbm, table_hbm, basis_hbm, out_ref,
    traces, table, basis, order, gathered, index_rows, bins, waves,
    core_in, chip_out, chip_in, slab_out, slab_in, part_out, part_in, edge_out, edge_in,
    table_sem, traces_sem, basis_sem, ib_s, ib_r, is_s, is_r,
    core_s, core_r, chip_s, chip_r, slab_s, slab_r, part_s, part_r, edge_s, edge_r,
):
    chips = beams // 2
    slab, beam = lax.axis_index("slab"), lax.axis_index("beam")
    core, chip = lax.rem(beam, 2), lax.div(beam, 2)
    other = 1 - core
    sibling = (slab, 2 * chip + other)
    chip_of = [lax.rem(chip + j, chips) for j in range(chips)]
    slab_of = [lax.rem(slab + k, slabs) for k in range(1, slabs)] + [slab]
    beam_peers = [(slab, lax.rem(beam + j, beams)) for j in range(1, beams)]
    slab_peers = [(s, beam) for s in slab_of[:-1]]

    load_table = pltpu.make_async_copy(table_hbm, table, table_sem)
    load_traces = pltpu.make_async_copy(traces_hbm, traces, traces_sem)
    load_basis = pltpu.make_async_copy(basis_hbm, basis, basis_sem)
    load_traces.start()
    load_table.start()
    barrier = pltpu.get_barrier_semaphore()
    for peer in beam_peers + slab_peers:
        pl.semaphore_signal(barrier, inc=1, device_id=peer, device_id_type=MESH)

    def send(src, dst, send_sem, recv_sem, device):
        copy = pltpu.make_async_remote_copy(
            src_ref=src, dst_ref=dst, send_sem=send_sem, recv_sem=recv_sem,
            device_id=device, device_id_type=MESH,
        )
        copy.start()
        return copy

    own_rows, depths = index_ref.shape
    gathered[slab, beam] = jnp.zeros(gathered.shape[2:], jnp.int32)
    gathered[slab, beam, :own_rows, :depths] = index_ref[...]
    shots, per_shot, doubled = traces.shape
    per_owner = shots // beams
    counts = [jnp.int32(0)] * beams
    places = []
    for i in range(shots):
        owner = lax.div(window_ref[i], WIN_OWN)
        place = jnp.int32(0)
        for b in range(beams):
            hit = owner == b
            place = jnp.where(hit, b * per_owner + counts[b], place)
            counts[b] = jnp.where(hit, counts[b] + 1, counts[b])
        places.append(place)
    for m in range(shots):
        shot = jnp.int32(0)
        for i in range(shots):
            shot = jnp.where(places[i] == m, jnp.int32(i), shot)
        order[m] = shot
    pl.semaphore_wait(barrier, len(beam_peers) + len(slab_peers))
    first = [
        send(gathered.at[slab, beam], gathered.at[slab, beam], ib_s.at[j], ib_r.at[j], peer)
        for j, peer in enumerate(beam_peers)
    ]

    half_f = doubled // 2
    slot_rows = lax.broadcasted_iota(jnp.int32, (K, per_shot), 0)

    def bin_shot(m, carry):
        shot = order[m]
        pick = (slot_rows == slot_ref[shot]).astype(F32).astype(BF16)
        binned = jnp.dot(pick, traces[shot], preferred_element_type=F32)
        re, im = binned[:, :half_f], binned[:, half_f:]
        both = jnp.concatenate(
            [jnp.concatenate([re, -im], axis=1), jnp.concatenate([im, re], axis=1)], axis=0
        )
        high = both.astype(BF16)
        bins[m, : 2 * K] = high
        bins[m, 2 * K :] = (both - high.astype(F32)).astype(BF16)
        return carry

    load_traces.wait()
    load_basis.start()
    lax.fori_loop(0, shots // 2, bin_shot, 0, unroll=2)
    for copy in first:
        copy.wait()
    second = [
        send(gathered.at[slab], gathered.at[slab], is_s.at[k], is_r.at[k], peer)
        for k, peer in enumerate(slab_peers)
    ]
    lax.fori_loop(shots // 2, shots, bin_shot, 0, unroll=2)
    load_table.wait()
    for copy in second:
        copy.wait()
    for b in range(beams):
        line = jnp.concatenate([gathered[s, b][:own_rows, :depths] for s in range(slabs)], axis=1)
        for w in range(WIN_OWN):
            index_rows[b * WIN_OWN + w] = line[w : w + 1]

    ray_rows = lax.broadcasted_iota(jnp.int32, (table.shape[0], slabs * depths), 0)

    def owner_waves(x, c):
        owner = 2 * x + c
        waves[c, x] = jnp.zeros(waves.shape[2:], F32)

        def one(t, carry):
            m = owner * per_owner + t
            w = window_ref[order[m]]
            pick = (ray_rows == index_rows[w]).astype(F32).astype(BF16)
            rays = lax.dot_general(
                pick, table[...], (((0,), (0,)), ((), ())), preferred_element_type=F32
            ).astype(BF16)
            parts = lax.dot_general(
                rays, bins[m], (((1,), (1,)), ((), ())), preferred_element_type=F32
            )
            part = parts[:, : 2 * K] + parts[:, 2 * K :]
            for v in range(WIN_OWN):
                weight = jnp.where(w == owner * WIN_OWN + v, 1.0, 0.0)
                for s in range(slabs):
                    waves[c, x, s, v * depths : (v + 1) * depths, :] += (
                        weight * part[s * depths : (s + 1) * depths]
                    )
            return carry

        lax.fori_loop(0, per_owner, one, 0, unroll=2)

    core_copies = {}
    chip_copies = [[] for _ in slab_of]
    for j in list(range(1, chips)) + [0]:
        x = chip_of[j]
        owner_waves(x, other)
        core_copies[j] = send(
            waves.at[other, x], core_in.at[j], core_s.at[j], core_r.at[j], sibling
        )
        owner_waves(x, core)
        core_copies[j].wait_recv()
        if j == 0:
            continue
        for k, s in enumerate(slab_of):
            chip_out[k, j - 1] = (waves[core, x, s] + core_in[j, s]).astype(BF16)
            chip_copies[k].append(
                send(
                    chip_out.at[k, j - 1], chip_in.at[k, j - 1],
                    chip_s.at[k, j - 1], chip_r.at[k, j - 1], (slab, 2 * x + core),
                )
            )
    slab_copies = []
    total = None
    for k, s in enumerate(slab_of):
        total = waves[core, chip, s] + core_in[0, s]
        for j, copy in enumerate(chip_copies[k]):
            copy.wait_recv()
            total = total + chip_in[k, j].astype(F32)
        if k < slabs - 1:
            slab_out[k] = total.astype(BF16)
            slab_copies.append(
                send(slab_out.at[k], slab_in.at[k], slab_s.at[k], slab_r.at[k], (s, beam))
            )
    for k, copy in enumerate(slab_copies):
        copy.wait_recv()
        total = total + slab_in[k].astype(F32)
    wave = jnp.dot(
        total, slant[...], precision=lax.Precision.HIGHEST, preferred_element_type=F32
    )
    lateral = out_ref.shape[1]
    rows = [wave[w * depths : (w + 1) * depths] for w in range(WIN_OWN)]
    mixed = []
    for lo in (0, P_SIZE):
        part = jnp.concatenate([r[:, lo : lo + P_SIZE] for r in rows], axis=1)
        high = part.astype(BF16)
        low = (part - high.astype(F32))
        mixed.append(jnp.concatenate([high.astype(F32), low], axis=0).astype(BF16))
    load_basis.wait()

    def terms(owner):
        cols = pl.ds(pl.multiple_of(owner * lateral, lateral), lateral)
        both = jnp.dot(mixed[0], basis[0, :, cols], preferred_element_type=F32)
        both += jnp.dot(mixed[1], basis[1, :, cols], preferred_element_type=F32)
        return both[:depths] + both[depths:]

    order = list(range(1, chips)) + [0]
    part_copies = {}
    for j in order:
        part_out[j] = terms(2 * chip_of[j] + other)
        part_copies[j] = send(
            part_out.at[j], part_in.at[j], part_s.at[j], part_r.at[j], sibling
        )
    edge_copies = []
    half = lateral // 2
    for j in range(1, chips):
        value = terms(2 * chip_of[j] + core)
        part_copies[j].wait_recv()
        value = value + part_in[j]
        edge_out[j - 1] = jnp.concatenate([value[:, :half], value[:, half:]], axis=0).astype(BF16)
        edge_copies.append(
            send(
                edge_out.at[j - 1], edge_in.at[j - 1], edge_s.at[j - 1], edge_r.at[j - 1],
                (slab, 2 * chip_of[j] + core),
            )
        )
    value = terms(beam)
    part_copies[0].wait_recv()
    out_ref[...] = value + part_in[0]
    for j, copy in enumerate(edge_copies):
        copy.wait_recv()
        edge = edge_in[j].astype(F32)
        out_ref[:, :half] += edge[:depths]
        out_ref[:, half:] += edge[depths:]
    sent = list(core_copies.values()) + slab_copies + list(part_copies.values()) + edge_copies
    for row in chip_copies:
        sent += row
    for copy in sent:
        copy.wait_send()


def body(traces, shot_window, trace_slot, ray_phase, ray_index, beam_basis):
    shots, per_shot, doubled = traces.shape
    beams = lax.axis_size("beam")
    slabs = lax.axis_size("slab")
    scale = (shots * slabs * beams * per_shot / (WIN_OWN * beams)) ** (-0.5)
    own_rows, depths = ray_index.shape
    chips = beams // 2
    lateral = beam_basis.shape[2] // beams
    rows = WIN_OWN * depths
    wide = 2 * K
    hops = max(chips - 1, 1)
    vmem = pl.BlockSpec(memory_space=pltpu.VMEM)
    smem = pl.BlockSpec(memory_space=pltpu.SMEM)
    hbm = pl.BlockSpec(memory_space=pl.ANY)
    dma = pltpu.SemaphoreType.DMA
    block = (-(-own_rows // 8) * 8, -(-depths // 128) * 128)
    return pl.pallas_call(
        functools.partial(migrate_kernel, slabs, beams),
        out_shape=jax.ShapeDtypeStruct((depths, lateral), F32),
        in_specs=[smem, vmem, vmem, vmem, hbm, hbm, hbm],
        out_specs=vmem,
        scratch_shapes=[
            pltpu.VMEM(traces.shape, BF16),
            pltpu.VMEM(ray_phase.shape, BF16),
            pltpu.VMEM(beam_basis.shape, BF16),
            pltpu.SMEM((shots,), jnp.int32),
            pltpu.VMEM((slabs, beams) + block, jnp.int32),
            pltpu.VMEM((beams * WIN_OWN, 1, slabs * depths), jnp.int32),
            pltpu.VMEM((shots, 4 * K, doubled), BF16),
            pltpu.VMEM((2, chips, slabs, rows, wide), F32),
            pltpu.VMEM((chips, slabs, rows, wide), F32),
            pltpu.VMEM((slabs, hops, rows, wide), BF16),
            pltpu.VMEM((slabs, hops, rows, wide), BF16),
            pltpu.VMEM((slabs, rows, wide), BF16),
            pltpu.VMEM((slabs, rows, wide), BF16),
            pltpu.VMEM((chips, depths, lateral), F32),
            pltpu.VMEM((chips, depths, lateral), F32),
            pltpu.VMEM((hops, 2 * depths, lateral // 2), BF16),
            pltpu.VMEM((hops, 2 * depths, lateral // 2), BF16),
            dma(()), dma(()), dma(()),
            dma((beams,)), dma((beams,)),
            dma((slabs,)), dma((slabs,)),
            dma((chips,)), dma((chips,)),
            dma((slabs, hops)), dma((slabs, hops)),
            dma((slabs,)), dma((slabs,)),
            dma((chips,)), dma((chips,)),
            dma((hops,)), dma((hops,)),
        ],
        compiler_params=pltpu.CompilerParams(
            collective_id=0, has_side_effects=True, vmem_limit_bytes=56 * 1024 * 1024
        ),
        name="migrate",
    )(
        shot_window, trace_slot.reshape(shots, 1, per_shot), ray_index, slant_matrix(scale),
        traces, ray_phase, beam_basis,
    )


def solution(mesh):
    in_specs = (
        P(("slab", "beam"), None, None),
        P(("slab", "beam")),
        P(("slab", "beam"), None),
        P(),
        P("beam", "slab"),
        P(None, "beam", None),
    )
    out_specs = P("slab", "beam")
    return jax.shard_map(body, mesh=mesh, in_specs=in_specs, out_specs=out_specs, check_vma=False)
```

time: 49.8 us -> 36.9 us (0.74)
  Pallas kernels: 41.8 us -> 35.1 us
  local copies, waits for them, and re-layouts: 7.61 us -> 1.62 us
    pallas_call x3 -> x1, Pallas kernels: 41.8 us -> 35.1 us  [body(): pl.pallas_call(functools.partial(migrate_kernel, slabs, beams), out_shape...]
    unnamed x11 -> x1, local copies, waits for them, and re-layouts: 5.26 us -> 1.62 us
    pad x1 -> x0, local copies, waits for them, and re-layouts: 1.31 us -> none  [gather_index(): mine = jnp.pad(ray_index, ((0, block[0] - rows), (0, block[1] - depths)))]
    transpose x2 -> x0, local copies, waits for them, and re-layouts: 0.94 us -> none  [gather_index(): out = out[:, :, :rows, :depths].transpose(1, 2, 0, 3)]
where the time goes in v3:
time: 36.9 us; the launch traced here: 36.7 us
  Pallas kernels  35.1 us (95%)
  local copies, waits for them, and re-layouts  1.62 us (4%)
    pallas_call x1, Pallas kernels, body(): pl.pallas_call(functools.partial(migrate_kernel, slabs, beams), out_shape...  35.1 us
    unnamed x1, local copies, waits for them, and re-layouts  1.62 us

profile of v3, /device:TPU:0, one launch (start us, length us, event | category | flops | bytes accessed | tf_op | source)
XLA Modules:
  0.0 36.7 jit_solution(18089709940740026546)
XLA Ops:
  0.0 35.1 %migrate.1 = f32[24,2048]{1,0:T(8,128)} custom-call(s32[16]{0:T(128)} %window_ref.1, s32[16,1,128]{2,1,0:T(1,128)} %bitcast.1, s32[4,24]{1,0:T(4,128)} %index_ref.1, f32[128,128]{1,0:T(8,128)} %constant.2.clone.slant, bf16[16,128,1024]{2,1,0:T(8,128)(2,1)} %traces_hbm.1, bf16[256,1024]{1,0:T(8,128)(2,1)} %table_hbm.1, bf16[2,256,8192]{2,1,0:T(8,128)(2,1)} %basis_hbm.1), custom_call_target="tpu_custom_call" | custom-call | tf_op jit(solution)/shard_map/migrate/pallas_call | solution.py:252
  35.1 1.6 %copy.9 = f32[24,2048]{1,0:T(8,128)} copy(f32[24,2048]{1,0:T(8,128)} %migrate.1) | data formatting | bytes 393216

commit v4 on v3

--- a/solution.py
+++ b/solution.py
@@ -25,7 +25,7 @@
 
 def migrate_kernel(
     slabs, beams, window_ref, slot_ref, index_ref, slant, traces_hbm, table_hbm, basis_hbm, out_ref,
-    traces, table, basis, order, gathered, index_rows, bins, waves,
+    traces, table, basis, order, gathered, index_rows, products, waves,
     core_in, chip_out, chip_in, slab_out, slab_in, part_out, part_in, edge_out, edge_in,
     table_sem, traces_sem, basis_sem, ib_s, ib_r, is_s, is_r,
     core_s, core_r, chip_s, chip_r, slab_s, slab_r, part_s, part_r, edge_s, edge_r,
@@ -95,21 +95,32 @@
             [jnp.concatenate([re, -im], axis=1), jnp.concatenate([im, re], axis=1)], axis=0
         )
         high = both.astype(BF16)
-        bins[m, : 2 * K] = high
-        bins[m, 2 * K :] = (both - high.astype(F32)).astype(BF16)
+        low = (both - high.astype(F32)).astype(BF16)
+        parts = lax.dot_general(
+            table[...],
+            jnp.concatenate([high, low], axis=0),
+            (((1,), (1,)), ((), ())),
+            preferred_element_type=F32,
+        )
+        part = parts[:, : 2 * K] + parts[:, 2 * K :]
+        base = lax.div(m, per_owner) * WIN_OWN
+        for v in range(WIN_OWN):
+            weight = jnp.where(window_ref[shot] == base + v, 1.0, 0.0)
+            products[base + v] += weight * part
         return carry
 
+    products[...] = jnp.zeros(products.shape, F32)
+    load_table.wait()
     load_traces.wait()
     load_basis.start()
-    lax.fori_loop(0, shots // 2, bin_shot, 0, unroll=2)
+    lax.fori_loop(0, shots // 2, bin_shot, 0, unroll=4)
     for copy in first:
         copy.wait()
     second = [
         send(gathered.at[slab], gathered.at[slab], is_s.at[k], is_r.at[k], peer)
         for k, peer in enumerate(slab_peers)
     ]
-    lax.fori_loop(shots // 2, shots, bin_shot, 0, unroll=2)
-    load_table.wait()
+    lax.fori_loop(shots // 2, shots, bin_shot, 0, unroll=4)
     for copy in second:
         copy.wait()
     for b in range(beams):
@@ -121,28 +132,23 @@
 
     def owner_waves(x, c):
         owner = 2 * x + c
-        waves[c, x] = jnp.zeros(waves.shape[2:], F32)
-
-        def one(t, carry):
-            m = owner * per_owner + t
-            w = window_ref[order[m]]
+        for v in range(WIN_OWN):
+            w = owner * WIN_OWN + v
             pick = (ray_rows == index_rows[w]).astype(F32).astype(BF16)
-            rays = lax.dot_general(
-                pick, table[...], (((0,), (0,)), ((), ())), preferred_element_type=F32
-            ).astype(BF16)
+            value = products[w]
+            high = value.astype(BF16)
+            low = (value - high.astype(F32)).astype(BF16)
             parts = lax.dot_general(
-                rays, bins[m], (((1,), (1,)), ((), ())), preferred_element_type=F32
+                pick,
+                jnp.concatenate([high, low], axis=1),
+                (((0,), (0,)), ((), ())),
+                preferred_element_type=F32,
             )
             part = parts[:, : 2 * K] + parts[:, 2 * K :]
-            for v in range(WIN_OWN):
-                weight = jnp.where(w == owner * WIN_OWN + v, 1.0, 0.0)
-                for s in range(slabs):
-                    waves[c, x, s, v * depths : (v + 1) * depths, :] += (
-                        weight * part[s * depths : (s + 1) * depths]
-                    )
-            return carry
-
-        lax.fori_loop(0, per_owner, one, 0, unroll=2)
+            for s in range(slabs):
+                waves[c, x, s, v * depths : (v + 1) * depths, :] = (
+                    part[s * depths : (s + 1) * depths]
+                )
 
     core_copies = {}
     chip_copies = [[] for _ in slab_of]
@@ -261,7 +267,7 @@
             pltpu.SMEM((shots,), jnp.int32),
             pltpu.VMEM((slabs, beams) + block, jnp.int32),
             pltpu.VMEM((beams * WIN_OWN, 1, slabs * depths), jnp.int32),
-            pltpu.VMEM((shots, 4 * K, doubled), BF16),
+            pltpu.VMEM((beams * WIN_OWN, ray_phase.shape[0], wide), F32),
             pltpu.VMEM((2, chips, slabs, rows, wide), F32),
             pltpu.VMEM((chips, slabs, rows, wide), F32),
             pltpu.VMEM((slabs, hops, rows, wide), BF16),

time: 36.9 us -> 34.6 us (0.938)
  Pallas kernels: 35.1 us -> 32.8 us
    pallas_call x1, Pallas kernels: 35.1 us -> 32.8 us  [body(): pl.pallas_call(functools.partial(migrate_kernel, slabs, beams), out_shape...]
where the time goes in v4:
time: 34.6 us; the launch traced here: 34.4 us
  Pallas kernels  32.8 us (95%)
  local copies, waits for them, and re-layouts  1.62 us (5%)
    pallas_call x1, Pallas kernels, body(): pl.pallas_call(functools.partial(migrate_kernel, slabs, beams), out_shape...  32.8 us
    unnamed x1, local copies, waits for them, and re-layouts  1.62 us

profile of v4, /device:TPU:0, one launch (start us, length us, event | category | flops | bytes accessed | tf_op | source)
XLA Modules:
  0.0 34.4 jit_solution(4147917287656595134)
XLA Ops:
  0.0 32.8 %migrate.1 = f32[24,2048]{1,0:T(8,128)} custom-call(s32[16]{0:T(128)} %window_ref.1, s32[16,1,128]{2,1,0:T(1,128)} %bitcast.1, s32[4,24]{1,0:T(4,128)} %index_ref.1, f32[128,128]{1,0:T(8,128)} %constant.2.clone.slant, bf16[16,128,1024]{2,1,0:T(8,128)(2,1)} %traces_hbm.1, bf16[256,1024]{1,0:T(8,128)(2,1)} %table_hbm.1, bf16[2,256,8192]{2,1,0:T(8,128)(2,1)} %basis_hbm.1), custom_call_target="tpu_custom_call" | custom-call | tf_op jit(solution)/shard_map/migrate/pallas_call | solution.py:258
  32.8 1.6 %copy.9 = f32[24,2048]{1,0:T(8,128)} copy(f32[24,2048]{1,0:T(8,128)} %migrate.1) | data formatting | bytes 393216

commit v5 on v4

--- a/solution.py
+++ b/solution.py
@@ -113,14 +113,14 @@
     load_table.wait()
     load_traces.wait()
     load_basis.start()
-    lax.fori_loop(0, shots // 2, bin_shot, 0, unroll=4)
+    lax.fori_loop(0, shots // 4, bin_shot, 0, unroll=4)
     for copy in first:
         copy.wait()
     second = [
         send(gathered.at[slab], gathered.at[slab], is_s.at[k], is_r.at[k], peer)
         for k, peer in enumerate(slab_peers)
     ]
-    lax.fori_loop(shots // 2, shots, bin_shot, 0, unroll=4)
+    lax.fori_loop(shots // 4, shots, bin_shot, 0, unroll=4)
     for copy in second:
         copy.wait()
     for b in range(beams):

time: 34.6 us -> 34.6 us (level)
  no operation moved by 1% of the time
where the time goes in v5:
time: 34.6 us; the launch traced here: 34.4 us
  Pallas kernels  32.8 us (95%)
  local copies, waits for them, and re-layouts  1.62 us (5%)
    pallas_call x1, Pallas kernels, body(): pl.pallas_call(functools.partial(migrate_kernel, slabs, beams), out_shape...  32.8 us
    unnamed x1, local copies, waits for them, and re-layouts  1.62 us

profile of v5, /device:TPU:0, one launch (start us, length us, event | category | flops | bytes accessed | tf_op | source)
XLA Modules:
  0.0 34.4 jit_solution(17968367032967841848)
XLA Ops:
  0.0 32.8 %migrate.1 = f32[24,2048]{1,0:T(8,128)} custom-call(s32[16]{0:T(128)} %window_ref.1, s32[16,1,128]{2,1,0:T(1,128)} %bitcast.1, s32[4,24]{1,0:T(4,128)} %index_ref.1, f32[128,128]{1,0:T(8,128)} %constant.2.clone.slant, bf16[16,128,1024]{2,1,0:T(8,128)(2,1)} %traces_hbm.1, bf16[256,1024]{1,0:T(8,128)(2,1)} %table_hbm.1, bf16[2,256,8192]{2,1,0:T(8,128)(2,1)} %basis_hbm.1), custom_call_target="tpu_custom_call" | custom-call | tf_op jit(solution)/shard_map/migrate/pallas_call | solution.py:258
  32.8 1.6 %copy.9 = f32[24,2048]{1,0:T(8,128)} copy(f32[24,2048]{1,0:T(8,128)} %migrate.1) | data formatting | bytes 393216
